TPU v7x, 32 devices: a whole 2x2x4 slice. The times are simulated.
32 devices in a mesh: groups: 2 (over y), blk: 4 (over x, core), sub: 4 (over z).
Axes of the slice: x: 2, y: 2, z: 4, core: 2. Of those that a mesh axis runs over, the one named last changes fastest.
Arguments:
- velocity: float32 [2, 512, 1024], P(None, ('groups', 'blk', 'sub')), parts along dimension 1, may hold values from -6 to 6
- stress: float32 [3, 512, 1024], P(None, ('groups', 'blk', 'sub')), parts along dimension 1, may hold values from -6 to 6
- ice_mass: float32 [512, 1024], P(('groups', 'blk', 'sub')), parts along dimension 0, may hold values from 0.5 to 3
- strength: float32 [512, 1024], P(('groups', 'blk', 'sub')), parts along dimension 0, may hold values from 0.3 to 3
- coriolis: float32 [512, 1024], P(('groups', 'blk', 'sub')), parts along dimension 0, may hold values from -1.5 to 1.5
- air_stress: float32 [2, 512, 1024], P(None, ('groups', 'blk', 'sub')), parts along dimension 1, may hold values from -4 to 4
- ocean_current: float32 [1536, 2, 1024], P(('groups', 'blk', 'sub')), parts along dimension 0, may hold values from -6 to 6
- neighbours: int32 [512, 4], P(('groups', 'blk', 'sub')), parts along dimension 0, may hold values from -1 to 255, as said below
- ocean_tile: int32 [512], P(('groups', 'blk', 'sub')), parts along dimension 0, may hold values from 0 to 767, as said below
Outputs:
- velocity_out: float32 [2, 512, 1024], P(None, ('groups', 'blk', 'sub')), parts along dimension 1
- stress_out: float32 [3, 512, 1024], P(None, ('groups', 'blk', 'sub')), parts along dimension 1
There are 2 independent parts, one for each index of `groups`. A program takes and returns all parts, laid end to end along the dimension named above; each array names one. Nothing has to cross between parts.
Inputs may be any that keep to these rules, and one draw needn't show every extreme that they name: Block b is held by device b // 16 in the order of blk+sub. The relation is symmetric: neighbours[b, 0] = a exactly when neighbours[a, 2] = b, and neighbours[b, 1] = a exactly when neighbours[a, 3] = b. The west and south neighbours of one device's blocks, counted together, lie on any one device at most 4 times, and so do their east and north neighbours; some device reaches 4. No block is its own neighbour. `ocean_tile`: no two blocks name the same tile. Tile t is held by device t // 48, which differs from the device holding the block only in its index along sub. One device's blocks name at most 8 tiles of any one device, and some device reaches 8.
All inputs are finite; a program needn't handle non-finite values.
Results may differ from a plain program's by a relative error of at most 0.00002.
Values sent between devices are 32-bit elements; how exact they have to be, the bound alone decides.
A program may use at most 64 MiB of HBM per device.

v0:
```python
import functools

import jax
import jax.numpy as jnp
from jax import lax
from jax.experimental import pallas as pl
from jax.experimental.pallas import tpu as pltpu
from jax.sharding import PartitionSpec as P

SIDE = 32
SUBCYCLES = 8
LANES = 128
CHUNKS = 8

DELTA_FLOOR = 0.01
RELAX = 0.3
SPEED_FLOOR = 0.01
MESH = pl.DeviceIdType.MESH
F32 = jnp.float32


def roll(x, shift):
    shift = shift % LANES
    return x if shift == 0 else pltpu.roll(x, shift, 1)


def lanes_like(x):
    return lax.broadcasted_iota(jnp.int32, x.shape, 1)


def gather_edges(col_a, col_b, row_a, row_b, col_lane, row_lane):
    lane = lanes_like(row_a)
    inner = lane % SIDE
    quarter = lane // SIDE
    out = jnp.zeros_like(row_a)
    for base, chunks in ((0, col_a), (8, col_b)):
        for k in range(CHUNKS):
            out = jnp.where(inner == base + k, roll(chunks[k], base + k - col_lane), out)
    for base, row in ((16, row_a), (24, row_b)):
        for c in range(4):
            there = (quarter == c) & (inner >= base) & (inner < base + 8)
            out = jnp.where(there, roll(row, 24 * c + base - row_lane), out)
    return out


def column_to(edges, base, k, col_lane):
    return roll(edges, col_lane - base - k)


def row_to(edges, base, row_lane):
    lane = lanes_like(edges)
    out = roll(edges, row_lane - base)
    for c in range(1, 4):
        moved = roll(edges, row_lane - base - 24 * c)
        out = jnp.where(lane >= row_lane + 8 * c, moved, out)
    return out


def chunk(k):
    return pl.ds(LANES * k, LANES)


def repeat(start, stop, body):
    if stop - start <= 64:
        for i in range(start, stop):
            body(i)
    else:

        def step(i, carry):
            body(i)
            return carry

        lax.fori_loop(start, stop, step, 0)


def kernel(
    sizes,
    plan,
    requests,
    vel_in,
    stress_in,
    mass,
    strength,
    coriolis,
    air,
    ocean,
    vel,
    stress,
    edges,
    borders,
    v_pack,
    v_recv,
    s_pack,
    s_recv,
    asked,
    asked_s,
    ans_pack,
    ans_recv,
    cur,
    consts,
    v_send_sem,
    v_recv_sem,
    s_send_sem,
    s_recv_sem,
    q_send_sem,
    q_recv_sem,
    a_send_sem,
    a_recv_sem,
    local_sem,
):
    n, owners, cap, tcap, blocks = sizes
    group, blk, sub = lax.axis_index("groups"), lax.axis_index("blk"), lax.axis_index("sub")
    me = blk * owners + sub

    def peer(o):
        d = lax.rem(me + o, n)
        return (group, d // owners, lax.rem(d, owners))

    def sub_peer(o):
        return (group, blk, lax.rem(sub + o + owners, owners))

    barrier = pltpu.get_barrier_semaphore()
    repeat(1, n, lambda o: pl.semaphore_signal(barrier, inc=1, device_id=peer(o), device_id_type=MESH))
    pl.semaphore_wait(barrier, n - 1)

    def request_copy(o):
        return pltpu.make_async_remote_copy(
            src_ref=requests.at[o],
            dst_ref=asked.at[o],
            send_sem=q_send_sem.at[o],
            recv_sem=q_recv_sem.at[o],
            device_id=sub_peer(o),
            device_id_type=MESH,
        )

    def answer_copy(o):
        return pltpu.make_async_remote_copy(
            src_ref=ans_pack.at[pl.ds(o * tcap, tcap)],
            dst_ref=ans_recv.at[pl.ds(o * tcap, tcap)],
            send_sem=a_send_sem.at[o],
            recv_sem=a_recv_sem.at[o],
            device_id=sub_peer(-o),
            device_id_type=MESH,
        )

    for o in range(1, owners):
        request_copy(o).start()

    slots = n * cap
    v_src, s_src, v_land, s_land, t_land = 0, slots, 2 * slots, 2 * slots + 2 * blocks, 2 * slots + 4 * blocks
    remote = pl.ds(cap, slots - cap)

    def trade(first, pack, recv, send_sem, recv_sem):
        def fill(s):
            pack[s] = edges[pl.ds(plan[first + s], 1), :]

        def fill_own(s):
            recv[s] = edges[pl.ds(plan[first + s], 1), :]

        repeat(0, cap, fill_own)
        repeat(cap, slots, fill)

        def send(o):
            where = pl.ds(o * cap, cap)
            pltpu.make_async_remote_copy(
                src_ref=pack.at[where],
                dst_ref=recv.at[where],
                send_sem=send_sem,
                recv_sem=recv_sem,
                device_id=peer(o),
                device_id_type=MESH,
            ).start()

        repeat(1, n, send)

    def wait_all(ref, sem):
        pltpu.make_async_copy(ref.at[remote], ref.at[remote], sem).wait()

    def land(first, recv):
        for b in range(blocks):
            from_col = recv[plan[first + 2 * b]]
            from_row = recv[plan[first + 2 * b + 1]]
            inner = lanes_like(from_col) % SIDE
            borders[pl.ds(b, 1), :] = jnp.where(inner < 16, from_col, from_row)
        return borders[...]

    def send_velocity(u, v):
        edges[...] = gather_edges(u, v, u[0], v[0], 0, 0)
        trade(v_src, v_pack, v_recv, v_send_sem, v_recv_sem)

    def stress_step(source):
        u = [vel_in[0, :, chunk(k)] if source else vel[0, :, chunk(k)] for k in range(CHUNKS)]
        v = [vel_in[1, :, chunk(k)] if source else vel[1, :, chunk(k)] for k in range(CHUNKS)]
        old = stress_in if source else stress
        wait_all(v_recv, v_recv_sem)
        got = land(v_land, v_recv)
        lane = lanes_like(got)
        inner = lane % SIDE
        ru = [roll(x, -SIDE) for x in u] + [row_to(got, 16, 96)]
        rv = [roll(x, -SIDE) for x in v] + [row_to(got, 24, 96)]
        xx, yy, xy = [], [], []
        for k in range(CHUNKS):
            u_e = jnp.where(inner == 31, column_to(got, 0, k, 31), roll(u[k], -1))
            v_e = jnp.where(inner == 31, column_to(got, 8, k, 31), roll(v[k], -1))
            u_n = jnp.where(lane < 96, ru[k], ru[k + 1])
            v_n = jnp.where(lane < 96, rv[k], rv[k + 1])
            along_x, along_y = u_e - u[k], v_n - v[k]
            diverge = along_x + along_y
            tension = along_x - along_y
            shearing = (u_n - u[k]) + (v_e - v[k])
            square = diverge * diverge + 0.25 * (tension * tension + shearing * shearing) + DELTA_FLOOR
            p = strength[:, chunk(k)]
            viscous = p * lax.rsqrt(square)
            s1, s2, s12 = (old[c, :, chunk(k)] for c in range(3))
            s1 = s1 + RELAX * (viscous * diverge - p - s1)
            s2 = s2 + RELAX * (0.25 * viscous * tension - s2)
            s12 = s12 + RELAX * (0.25 * viscous * shearing - s12)
            stress[0, :, chunk(k)] = s1
            stress[1, :, chunk(k)] = s2
            stress[2, :, chunk(k)] = s12
            xx.append(0.5 * (s1 + s2))
            yy.append(0.5 * (s1 - s2))
            xy.append(0.5 * s12)
        wait_all(v_pack, v_send_sem)
        edges[...] = gather_edges(xx, xy, yy[-1], xy[-1], 31, 96)
        trade(s_src, s_pack, s_recv, s_send_sem, s_recv_sem)

    def velocity_step(source, more):
        wait_all(s_recv, s_recv_sem)
        got = land(s_land, s_recv)
        lane = lanes_like(got)
        inner = lane % SIDE
        old_yy, old_xy = row_to(got, 16, 0), row_to(got, 24, 0)
        us, vs = [], []
        for k in range(CHUNKS):
            s1, s2, s12 = (stress[c, :, chunk(k)] for c in range(3))
            xx, yy, xy = 0.5 * (s1 + s2), 0.5 * (s1 - s2), 0.5 * s12
            xx_w = jnp.where(inner == 0, column_to(got, 0, k, 0), roll(xx, 1))
            xy_w = jnp.where(inner == 0, column_to(got, 8, k, 0), roll(xy, 1))
            new_yy, new_xy = roll(yy, SIDE), roll(xy, SIDE)
            yy_s = jnp.where(lane < SIDE, old_yy, new_yy)
            xy_s = jnp.where(lane < SIDE, old_xy, new_xy)
            old_yy, old_xy = new_yy, new_xy
            force_x = xx - xx_w + xy - xy_s
            force_y = xy - xy_w + yy - yy_s
            here = vel_in if source else vel
            u, v = here[0, :, chunk(k)], here[1, :, chunk(k)]
            uo, vo = cur[0, :, chunk(k)], cur[1, :, chunk(k)]
            inertia, r, cx, cy = (consts[c, :, chunk(k)] for c in range(4))
            dx, dy = uo - u, vo - v
            drag = jnp.sqrt(dx * dx + dy * dy + SPEED_FLOOR)
            a = inertia + drag
            gx = inertia * u + force_x + cx + drag * uo
            gy = inertia * v + force_y + cy + drag * vo
            inv = 1.0 / (a * a + r * r)
            u, v = (a * gx + r * gy) * inv, (a * gy - r * gx) * inv
            vel[0, :, chunk(k)] = u
            vel[1, :, chunk(k)] = v
            us.append(u)
            vs.append(v)
        wait_all(s_pack, s_send_sem)
        if more:
            send_velocity(us, vs)

    zero_row = jnp.zeros((1, LANES), F32)
    v_recv[slots] = zero_row
    s_recv[slots] = zero_row
    send_velocity(
        [vel_in[0, :, chunk(k)] for k in range(CHUNKS)], [vel_in[1, :, chunk(k)] for k in range(CHUNKS)]
    )

    asked[0] = requests[0]
    for o in range(1, owners):
        request_copy(o).wait()
    to_scalar = pltpu.make_async_copy(asked, asked_s, local_sem)
    to_scalar.start()
    to_scalar.wait()
    for o in range(owners):
        for t in range(tcap):
            (ans_pack if o else ans_recv)[o * tcap + t] = ocean[asked_s[o, 0, t]]
        if o:
            answer_copy(o).start()

    stress_step(True)

    for o in range(1, owners):
        answer_copy(o).wait()
    for b in range(blocks):
        row = ans_recv[plan[t_land + b]]
        cur[0, pl.ds(b, 1), :] = row[0:1]
        cur[1, pl.ds(b, 1), :] = row[1:2]
    for k in range(CHUNKS):
        m = mass[:, chunk(k)]
        r = m * coriolis[:, chunk(k)]
        consts[0, :, chunk(k)] = 2.0 * m
        consts[1, :, chunk(k)] = r
        consts[2, :, chunk(k)] = air[0, :, chunk(k)] - r * cur[1, :, chunk(k)]
        consts[3, :, chunk(k)] = air[1, :, chunk(k)] + r * cur[0, :, chunk(k)]

    velocity_step(True, True)

    def subcycle(_, carry):
        stress_step(False)
        velocity_step(False, True)
        return carry

    lax.fori_loop(0, SUBCYCLES - 2, subcycle, 0)
    stress_step(False)
    velocity_step(False, False)


def make_plan(neighbours, ocean_tile, sizes, tiles_dev):
    n, owners, cap, tcap, blocks = sizes
    sub = lax.axis_index("sub")
    me = lax.axis_index("blk") * owners + sub
    entry = jnp.arange(2 * blocks, dtype=jnp.int32)

    def sending(targets):
        t = targets.reshape(-1)
        away = jnp.where(t >= 0, (t // blocks - me) % n, n)
        ahead = (away[:, None] == away[None, :]) & (entry[None, :] < entry[:, None])
        place = away * cap + jnp.sum(ahead.astype(jnp.int32), axis=1)
        slot = jnp.arange(n * cap, dtype=jnp.int32)
        hit = (place[None, :] == slot[:, None]) & (away < n)[None, :]
        return jnp.sum(jnp.where(hit, (entry // 2)[None, :], 0), axis=1)

    def landing(sources):
        s = sources.reshape(-1)
        known = s >= 0
        away = jnp.where(known, (me - s // blocks) % n, n)
        key = s * 2 + entry % 2
        ahead = (away[:, None] == away[None, :]) & (key[None, :] < key[:, None])
        place = away * cap + jnp.sum(ahead.astype(jnp.int32), axis=1)
        return jnp.where(known, place, n * cap)

    away = (ocean_tile // tiles_dev - sub) % owners
    order = jnp.arange(blocks, dtype=jnp.int32)
    ahead = (away[:, None] == away[None, :]) & (order[None, :] < order[:, None])
    rank = jnp.sum(ahead.astype(jnp.int32), axis=1)
    place = away * tcap + rank
    lane = jnp.arange(LANES, dtype=jnp.int32)
    wanted = away * LANES + rank
    spots = jnp.arange(owners, dtype=jnp.int32)[:, None] * LANES + lane[None, :]
    hit = spots[:, :, None] == wanted[None, None, :]
    requests = jnp.sum(jnp.where(hit, (ocean_tile % tiles_dev)[None, None, :], 0), axis=2)
    plan = jnp.concatenate(
        [
            sending(neighbours[:, 0:2]),
            sending(neighbours[:, 2:4]),
            landing(neighbours[:, 2:4]),
            landing(neighbours[:, 0:2]),
            place,
        ]
    )
    return plan, requests.reshape(owners, 1, LANES)


def shards(
    velocity, stress, ice_mass, strength, coriolis, air_stress, ocean_current, neighbours, ocean_tile
):
    blocks = velocity.shape[1]
    n = lax.axis_size(("blk", "sub"))
    owners = lax.axis_size("sub")
    cap = max(2, 4 * blocks // n)
    tcap = max(1, 2 * blocks // owners)
    sizes = (n, owners, cap, tcap, blocks)
    cells = velocity.shape[2]
    plan, requests = make_plan(neighbours, ocean_tile, sizes, ocean_current.shape[0])
    slots = n * cap
    vmem = pl.BlockSpec(memory_space=pltpu.VMEM)
    dma = pltpu.SemaphoreType.DMA
    return pl.pallas_call(
        functools.partial(kernel, sizes),
        out_shape=(
            jax.ShapeDtypeStruct(velocity.shape, F32),
            jax.ShapeDtypeStruct(stress.shape, F32),
        ),
        in_specs=[pl.BlockSpec(memory_space=pltpu.SMEM)] + [vmem] * 8,
        out_specs=(vmem, vmem),
        scratch_shapes=[
            pltpu.VMEM((blocks, LANES), F32),
            pltpu.VMEM((blocks, LANES), F32),
            pltpu.VMEM((slots, 1, LANES), F32),
            pltpu.VMEM((slots + 1, 1, LANES), F32),
            pltpu.VMEM((slots, 1, LANES), F32),
            pltpu.VMEM((slots + 1, 1, LANES), F32),
            pltpu.VMEM((owners, 1, LANES), jnp.int32),
            pltpu.SMEM((owners, 1, LANES), jnp.int32),
            pltpu.VMEM((owners * tcap, 2, cells), F32),
            pltpu.VMEM((owners * tcap, 2, cells), F32),
            pltpu.VMEM((2, blocks, cells), F32),
            pltpu.VMEM((4, blocks, cells), F32),
            dma,
            dma,
            dma,
            dma,
            dma((owners,)),
            dma((owners,)),
            dma((owners,)),
            dma((owners,)),
            dma,
        ],
        compiler_params=pltpu.CompilerParams(collective_id=0, has_side_effects=True),
    )(plan, requests, velocity, stress, ice_mass, strength, coriolis, air_stress, ocean_current)


def solution(mesh):
    split = ("groups", "blk", "sub")
    placed = (
        P(None, split, None),
        P(None, split, None),
        P(split, None),
        P(split, None),
        P(split, None),
        P(None, split, None),
        P(split, None, None),
        P(split, None),
        P(split),
    )
    return jax.shard_map(
        shards,
        mesh=mesh,
        in_specs=placed,
        out_specs=(P(None, split, None), P(None, split, None)),
        check_vma=False,
    )
```

profile of v0, /device:TPU:0, one launch (start us, length us, event | category | flops | bytes accessed | tf_op | source)
XLA Modules:
  0.0 88.7 jit_solution(10449418895588625157)
XLA Ops:
  0.6 0.0 copy-start.2
  0.7 0.6 copy-done.2
  1.3 0.2 convert_reduce_fusion.4
  1.5 0.1 iota_add_fusion
  1.6 0.0 copy-start.1
  1.6 0.7 select_reduce_fusion
  2.3 0.0 copy-done.1
  2.3 0.1 copy.15
  2.4 0.1 reshape.433
  2.5 0.1 copy.16
  2.5 0.1 reshape.434
  2.7 0.2 convert_reduce_fusion.1
  2.9 0.2 convert_reduce_fusion.3
  3.1 0.2 convert_reduce_fusion.2
  3.3 0.1 select_reduce_fusion.1
  3.4 0.2 convert_reduce_fusion
  3.6 0.7 concatenate.3.plan
  4.2 82.2 %shard_map.104 = (f32[2,16,1024]{2,1,0:T(8,128)}, f32[3,16,1024]{2,1,0:T(8,128)}) custom-call(s32[208]{0:T(256)} %concatenate.3.plan, s32[4,1,128]{2,1,0:T(1,128)} %bitcast.1, f32[2,16,1024]{2,1,0:T(8,128)} %vel_in.1, f32[3,16,1024]{2,1,0:T(8,128)} %stress_in.1, f32[16,1024]{1,0:T(8,128)} %mass.1, f32[16,1024]{1,0:T(8,128)} %strength.1, ...), custom_call_target="tpu_custom_call" | custom-call | tf_op jit(solution)/shard_map/pallas_call | solution.py:372
  86.4 0.0 copy-start
  86.5 1.6 %copy.19 = f32[2,16,1024]{2,1,0:T(8,128)} copy(f32[2,16,1024]{2,1,0:T(8,128)} %get-tuple-element.25) | data formatting | bytes 262144
  88.1 0.0 copy-done
  88.1 0.7 copy.20
  (12 shorter events, 0.1 us)
Async XLA Ops:
  0.6 0.7 copy-start.2
  1.6 0.7 copy-start.1
  86.4 1.6 %copy-start = (f32[3,16,1024]{2,1,0:T(8,128)S(1)}, f32[3,16,1024]{2,1,0:T(8,128)}, u32[]{:S(2)}) copy-start(f32[3,16,1024]{2,1,0:T(8,128)} %get-tuple-element.26) | copy-start | bytes 589828
where the time goes:
time: 88.9 us; the launch traced here: 88.7 us
  Pallas kernels  82.2 us (92%)
  local copies, waits for them, and re-layouts  3.95 us (4%)
  other arithmetic  1.86 us (2%)
    pallas_call x1, Pallas kernels, shards(): pl.pallas_call(functools.partial(kernel, sizes), out_shape=(jax.ShapeDtyp...  82.2 us
    unnamed x8, local copies, waits for them, and re-layouts  2.95 us

commit v1 on v0

v1 whole, which is shorter than its diff:
```python
import functools

import jax
import jax.numpy as jnp
from jax import lax
from jax.experimental import pallas as pl
from jax.experimental.pallas import tpu as pltpu
from jax.sharding import PartitionSpec as P

SIDE = 32
SUBCYCLES = 8
LANES = 128
CHUNKS = 8

DELTA_FLOOR = 0.01
RELAX = 0.3
SPEED_FLOOR = 0.01
MESH = pl.DeviceIdType.MESH
F32 = jnp.float32


def roll(x, shift):
    shift = shift % LANES
    return x if shift == 0 else pltpu.roll(x, shift, 1)


def lanes_like(x):
    return lax.broadcasted_iota(jnp.int32, x.shape, 1)


def gather_edges(col_a, col_b, row_a, row_b, col_lane, row_lane):
    lane = lanes_like(row_a)
    inner = lane % SIDE
    quarter = lane // SIDE
    out = jnp.zeros_like(row_a)
    for base, chunks in ((0, col_a), (8, col_b)):
        for k in range(CHUNKS):
            out = jnp.where(inner == base + k, roll(chunks[k], base + k - col_lane), out)
    for base, row in ((16, row_a), (24, row_b)):
        for c in range(4):
            there = (quarter == c) & (inner >= base) & (inner < base + 8)
            out = jnp.where(there, roll(row, 24 * c + base - row_lane), out)
    return out


def column_to(edges, base, k, col_lane):
    return roll(edges, col_lane - base - k)


def row_to(edges, base, row_lane):
    lane = lanes_like(edges)
    out = roll(edges, row_lane - base)
    for c in range(1, 4):
        moved = roll(edges, row_lane - base - 24 * c)
        out = jnp.where(lane >= row_lane + 8 * c, moved, out)
    return out


def chunk(k):
    return pl.ds(LANES * k, LANES)


def repeat(start, stop, body):
    if stop - start <= 64:
        for i in range(start, stop):
            body(i)
    else:

        def step(i, carry):
            body(i)
            return carry

        lax.fori_loop(start, stop, step, 0)


def kernel(
    sizes,
    plan,
    table_row,
    vel_in,
    stress_in,
    mass,
    strength,
    coriolis,
    air,
    ocean,
    vel,
    stress,
    low_edges,
    high_edges,
    near,
    far,
    corners,
    corner_lane,
    corner_slot,
    halo,
    pack,
    recv_even,
    recv_odd,
    h_pack,
    h_recv,
    table,
    table_s,
    ans_pack,
    ans_recv,
    cur,
    consts,
    send_sem,
    recv_sem,
    h_send_sem,
    h_recv_sem,
    t_send_sem,
    t_recv_sem,
    a_send_sem,
    a_recv_sem,
    local_sem,
):
    n, owners, cap, tcap, blocks = sizes
    rows = cap + 1
    slots = n * cap
    zero_slot = n * rows
    group, blk, sub = lax.axis_index("groups"), lax.axis_index("blk"), lax.axis_index("sub")
    me = blk * owners + sub
    recv = (recv_even, recv_odd)
    low_src, high_src = 0, slots
    land = 2 * slots
    h_land = land + 4 * blocks
    t_land = h_land + 2 * blocks

    def peer(o):
        d = lax.rem(me + o, n)
        return (group, d // owners, lax.rem(d, owners))

    def sub_peer(o):
        return (group, blk, lax.rem(sub + o + owners, owners))

    def send_to(o, source, target, sent, received, device):
        return pltpu.make_async_remote_copy(
            src_ref=source,
            dst_ref=target,
            send_sem=sent,
            recv_sem=received,
            device_id=device,
            device_id_type=MESH,
        )

    def wait_all(ref, sem):
        pltpu.make_async_copy(ref, ref, sem).wait()

    def answer_copy(o):
        where = pl.ds(o * tcap, tcap)
        return send_to(
            o, ans_pack.at[where], ans_recv.at[where], a_send_sem.at[o], a_recv_sem.at[o], sub_peer(-o)
        )

    barrier = pltpu.get_barrier_semaphore()
    repeat(1, n, lambda o: pl.semaphore_signal(barrier, inc=1, device_id=peer(o), device_id_type=MESH))
    pl.semaphore_wait(barrier, n - 1)
    repeat(
        1, n, lambda o: send_to(o, table_row, table.at[o], t_send_sem, t_recv_sem, peer(o)).start()
    )

    def trade(u, v, parity):
        lane = lanes_like(u[0])
        block = lax.broadcasted_iota(jnp.int32, u[0].shape, 0)
        low = gather_edges(u, v, u[0], v[0], 0, 0)
        high = gather_edges(u, v, u[-1], v[-1], 31, 96)
        low_edges[0:blocks] = low
        low_edges[blocks : 2 * blocks] = roll(low, -16)
        high_edges[0:blocks] = high
        high_edges[blocks : 2 * blocks] = roll(high, 16)
        spread = jnp.zeros_like(low)
        for place, value in enumerate((u[0][:, 31:32], v[0][:, 31:32], u[-1][:, 96:97], v[-1][:, 96:97])):
            spread = jnp.where(lane == block + place * blocks, value, spread)
        corner_row = jnp.sum(spread, axis=0, keepdims=True)
        half = lax.broadcasted_iota(jnp.int32, (1, LANES), 1) % SIDE < 16
        into = recv[parity]

        def fill(o, target):
            for t in range(cap):
                low_row = low_edges[pl.ds(plan[low_src + o * cap + t], 1), :]
                high_row = high_edges[pl.ds(plan[high_src + o * cap + t], 1), :]
                target[o * rows + t] = jnp.where(half, low_row, high_row)
            target[o * rows + cap] = corner_row

        def fill_and_send(o):
            fill(o, pack)
            where = pl.ds(o * rows, rows)
            send_to(
                o, pack.at[where], into.at[where], send_sem.at[parity], recv_sem.at[parity], peer(o)
            ).start()

        repeat(1, n, fill_and_send)
        fill(0, into)

    remote = pl.ds(rows, (n - 1) * rows)

    def arrive(parity):
        wait_all(recv[parity].at[remote], recv_sem.at[parity])
        half = lax.broadcasted_iota(jnp.int32, (1, LANES), 1) % SIDE < 16
        for b in range(blocks):
            east, north, west, south = (recv[parity][plan[land + 4 * b + c]] for c in range(4))
            near[pl.ds(b, 1), :] = jnp.where(half, east, south)
            far[pl.ds(b, 1), :] = jnp.where(half, north, west)
            corners[0, pl.ds(b, 1), :] = recv[parity][corner_slot[b]]
            corners[1, pl.ds(b, 1), :] = recv[parity][corner_slot[blocks + b]]
        straight, crossed = near[0:blocks], far[0:blocks]
        half = lanes_like(straight) % SIDE < 16
        low = jnp.where(half, straight, roll(crossed, 16))
        high = jnp.where(half, roll(crossed, -16), straight)
        return low, high

    def corner_value(which, place):
        x = corners[which]
        hit = lanes_like(x) == corner_lane[which] + place * blocks
        return jnp.sum(jnp.where(hit, x, 0.0), axis=1, keepdims=True)

    def advance(stress_old, u, v, u_e, v_e, u_n, v_n, p):
        along_x, along_y = u_e - u, v_n - v
        diverge = along_x + along_y
        tension = along_x - along_y
        shearing = (u_n - u) + (v_e - v)
        square = diverge * diverge + 0.25 * (tension * tension + shearing * shearing) + DELTA_FLOOR
        viscous = p * lax.rsqrt(square)
        s1, s2, s12 = stress_old
        return (
            s1 + RELAX * (viscous * diverge - p - s1),
            s2 + RELAX * (0.25 * viscous * tension - s2),
            s12 + RELAX * (0.25 * viscous * shearing - s12),
        )

    def halo_step(high):
        lane = lanes_like(high)
        inner = lane % SIDE
        column = inner < 16

        def ahead(x, north_west, south_east):
            up = jnp.where(lane < 96, roll(x, -32), roll(x, 95))
            up = jnp.where(lane == 103, north_west, up)
            right = jnp.where(inner == 23, roll(x, -25), roll(x, -1))
            right = jnp.where(lane == 119, south_east, right)
            return jnp.where(column, up, right)

        mine = low_edges[0:blocks]
        u, v = high, roll(high, -8)
        mine_u, mine_v = mine, roll(mine, -8)
        ahead_u = ahead(u, corner_value(0, 0), corner_value(1, 2))
        ahead_v = ahead(v, corner_value(0, 1), corner_value(1, 3))
        s1, s2, s12 = advance(
            (halo[0], halo[1], halo[2]),
            u,
            v,
            jnp.where(column, mine_u, ahead_u),
            jnp.where(column, mine_v, ahead_v),
            jnp.where(column, ahead_u, mine_u),
            jnp.where(column, ahead_v, mine_v),
            halo[3],
        )
        halo[0], halo[1], halo[2] = s1, s2, s12
        return 0.5 * (s1 + s2), 0.5 * (s1 - s2), 0.5 * s12

    def subcycle(parity, first, last):
        here, old = (vel_in, stress_in) if first else (vel, stress)
        low, high = arrive(parity)
        if first:
            settle()
        halo_xx, halo_yy, halo_xy = halo_step(high)
        lane = lanes_like(low)
        inner = lane % SIDE
        us = [here[0, :, chunk(k)] for k in range(CHUNKS)]
        vs = [here[1, :, chunk(k)] for k in range(CHUNKS)]
        old_yy, old_xy = row_to(halo_yy, 16, 0), row_to(halo_xy, 16, 0)
        next_u, next_v = roll(us[0], -SIDE), roll(vs[0], -SIDE)
        new_u, new_v = [], []
        for k in range(CHUNKS):
            u, v = us[k], vs[k]
            this_u, this_v = next_u, next_v
            if k + 1 < CHUNKS:
                next_u, next_v = roll(us[k + 1], -SIDE), roll(vs[k + 1], -SIDE)
            else:
                next_u, next_v = row_to(low, 16, 96), row_to(low, 24, 96)
            s1, s2, s12 = advance(
                [old[c, :, chunk(k)] for c in range(3)],
                u,
                v,
                jnp.where(inner == 31, column_to(low, 0, k, 31), roll(u, -1)),
                jnp.where(inner == 31, column_to(low, 8, k, 31), roll(v, -1)),
                jnp.where(lane < 96, this_u, next_u),
                jnp.where(lane < 96, this_v, next_v),
                strength[:, chunk(k)],
            )
            stress[0, :, chunk(k)] = s1
            stress[1, :, chunk(k)] = s2
            stress[2, :, chunk(k)] = s12
            xx, yy, xy = 0.5 * (s1 + s2), 0.5 * (s1 - s2), 0.5 * s12
            xx_w = jnp.where(inner == 0, column_to(halo_xx, 0, k, 0), roll(xx, 1))
            xy_w = jnp.where(inner == 0, column_to(halo_xy, 0, k, 0), roll(xy, 1))
            new_yy, new_xy = roll(yy, SIDE), roll(xy, SIDE)
            yy_s = jnp.where(lane < SIDE, old_yy, new_yy)
            xy_s = jnp.where(lane < SIDE, old_xy, new_xy)
            old_yy, old_xy = new_yy, new_xy
            force_x = xx - xx_w + xy - xy_s
            force_y = xy - xy_w + yy - yy_s
            uo, vo = cur[0, :, chunk(k)], cur[1, :, chunk(k)]
            inertia, r, cx, cy = (consts[c, :, chunk(k)] for c in range(4))
            dx, dy = uo - u, vo - v
            drag = jnp.sqrt(dx * dx + dy * dy + SPEED_FLOOR)
            a = inertia + drag
            gx = inertia * u + force_x + cx + drag * uo
            gy = inertia * v + force_y + cy + drag * vo
            inv = 1.0 / (a * a + r * r)
            u, v = (a * gx + r * gy) * inv, (a * gy - r * gx) * inv
            vel[0, :, chunk(k)] = u
            vel[1, :, chunk(k)] = v
            new_u.append(u)
            new_v.append(v)
        wait_all(pack.at[remote], send_sem.at[parity])
        if not last:
            trade(new_u, new_v, 1 - parity)

    def settle():
        wait_all(h_recv.at[pl.ds(2 * cap, 2 * (slots - cap))], h_recv_sem)
        wait_all(h_pack.at[pl.ds(2 * cap, 2 * (slots - cap))], h_send_sem)
        half = lax.broadcasted_iota(jnp.int32, (1, LANES), 1) % SIDE < 16
        for b in range(blocks):
            west, south = 2 * plan[h_land + 2 * b], 2 * plan[h_land + 2 * b + 1]
            near[pl.ds(b, 1), :] = jnp.where(half, h_recv[west], h_recv[south])
            far[pl.ds(b, 1), :] = jnp.where(half, h_recv[west + 1], h_recv[south + 1])
        first, second = near[0:blocks], far[0:blocks]
        halo[0], halo[1] = first, roll(first, -8)
        halo[2], halo[3] = second, roll(second, -8)
        for o in range(1, owners):
            answer_copy(o).wait()
        for b in range(blocks):
            row = ans_recv[plan[t_land + b]]
            cur[0, pl.ds(b, 1), :] = row[0:1]
            cur[1, pl.ds(b, 1), :] = row[1:2]
        for k in range(CHUNKS):
            m = mass[:, chunk(k)]
            r = m * coriolis[:, chunk(k)]
            consts[0, :, chunk(k)] = 2.0 * m
            consts[1, :, chunk(k)] = r
            consts[2, :, chunk(k)] = air[0, :, chunk(k)] - r * cur[1, :, chunk(k)]
            consts[3, :, chunk(k)] = air[1, :, chunk(k)] + r * cur[0, :, chunk(k)]

    zero_row = jnp.zeros((1, LANES), F32)
    recv_even[zero_slot] = zero_row
    recv_odd[zero_slot] = zero_row
    h_recv[2 * slots] = zero_row
    h_recv[2 * slots + 1] = zero_row
    trade([vel_in[0, :, chunk(k)] for k in range(CHUNKS)], [vel_in[1, :, chunk(k)] for k in range(CHUNKS)], 0)

    s1, s2, s12 = ([stress_in[c, :, chunk(k)] for k in range(CHUNKS)] for c in range(3))
    p = [strength[:, chunk(k)] for k in range(CHUNKS)]
    first = gather_edges(s1, s2, s1[-1], s2[-1], 31, 96)
    second = gather_edges(s12, p, s12[-1], p[-1], 31, 96)
    for copy in range(2):
        near[copy * blocks : (copy + 1) * blocks] = first
        far[copy * blocks : (copy + 1) * blocks] = second

    def fill_halo(o, target):
        for t in range(cap):
            s = plan[high_src + o * cap + t]
            target[2 * (o * cap + t)] = near[pl.ds(s, 1), :]
            target[2 * (o * cap + t) + 1] = far[pl.ds(s, 1), :]

    def send_halo(o):
        fill_halo(o, h_pack)
        where = pl.ds(2 * o * cap, 2 * cap)
        send_to(o, h_pack.at[where], h_recv.at[where], h_send_sem, h_recv_sem, peer(o)).start()

    repeat(1, n, send_halo)
    fill_halo(0, h_recv)

    table[0] = table_row[...]
    wait_all(table.at[pl.ds(1, n - 1)], t_recv_sem)
    wait_all(table.at[pl.ds(1, n - 1)], t_send_sem)
    to_scalar = pltpu.make_async_copy(table, table_s, local_sem)
    to_scalar.start()
    to_scalar.wait()
    for o in range(owners):
        holder = blk * owners + lax.rem(sub - o + owners, owners)
        slot = lax.rem(me - holder + n, n)
        for t in range(tcap):
            tile = ocean[table_s[slot, 0, 4 * blocks + o * tcap + t]]
            (ans_pack if o else ans_recv)[o * tcap + t] = tile
        if o:
            answer_copy(o).start()
    for b in range(blocks):
        for which in range(2):
            via = jnp.maximum(table_s[0, 0, 4 * b + which], 0)
            there = lax.rem(me - via // blocks + n, n)
            far_block = table_s[there, 0, 4 * lax.rem(via, blocks) + 3 - which]
            known = far_block >= 0
            far_block = jnp.maximum(far_block, 0)
            slot = lax.rem(me - far_block // blocks + n, n) * rows + cap
            corner_slot[which * blocks + b] = jnp.where(known, slot, zero_slot)
            corner_lane[which, pl.ds(b, 1), :] = jnp.full((1, LANES), lax.rem(far_block, blocks), jnp.int32)

    subcycle(0, True, False)

    def pair(_, carry):
        subcycle(1, False, False)
        subcycle(0, False, False)
        return carry

    lax.fori_loop(0, (SUBCYCLES - 2) // 2, pair, 0)
    subcycle(1, False, True)


def make_plan(neighbours, ocean_tile, sizes, tiles_dev):
    n, owners, cap, tcap, blocks = sizes
    sub = lax.axis_index("sub")
    me = lax.axis_index("blk") * owners + sub
    entry = jnp.arange(2 * blocks, dtype=jnp.int32)

    def sending(targets, content):
        t = targets.reshape(-1)
        away = jnp.where(t >= 0, (t // blocks - me) % n, n)
        ahead = (away[:, None] == away[None, :]) & (entry[None, :] < entry[:, None])
        place = away * cap + jnp.sum(ahead.astype(jnp.int32), axis=1)
        slot = jnp.arange(n * cap, dtype=jnp.int32)
        hit = (place[None, :] == slot[:, None]) & (away < n)[None, :]
        return jnp.sum(jnp.where(hit, content[None, :], 0), axis=1)

    def landing(sources):
        s = sources.reshape(-1)
        known = s >= 0
        away = jnp.where(known, (me - s // blocks) % n, n)
        key = s * 2 + entry % 2
        ahead = (away[:, None] == away[None, :]) & (key[None, :] < key[:, None])
        rank = jnp.sum(ahead.astype(jnp.int32), axis=1)
        main = jnp.where(known, away * (cap + 1) + rank, n * (cap + 1))
        return main.reshape(-1, 2), jnp.where(known, away * cap + rank, n * cap)

    away = (ocean_tile // tiles_dev - sub) % owners
    order = jnp.arange(blocks, dtype=jnp.int32)
    ahead = (away[:, None] == away[None, :]) & (order[None, :] < order[:, None])
    place = away * tcap + jnp.sum(ahead.astype(jnp.int32), axis=1)
    hit = jnp.arange(owners * tcap, dtype=jnp.int32)[:, None] == place[None, :]
    requests = jnp.sum(jnp.where(hit, (ocean_tile % tiles_dev)[None, :], 0), axis=1)
    row = jnp.concatenate([neighbours.reshape(-1), requests])
    row = jnp.pad(row, (0, LANES - row.shape[0])).reshape(1, LANES)
    from_east, _ = landing(neighbours[:, 2:4])
    from_west, halo_land = landing(neighbours[:, 0:2])
    kind = entry % 2
    plan = jnp.concatenate(
        [
            sending(neighbours[:, 0:2], entry // 2 + kind * blocks),
            sending(neighbours[:, 2:4], entry // 2 + (1 - kind) * blocks),
            jnp.concatenate([from_east, from_west], axis=1).reshape(-1),
            halo_land,
            place,
        ]
    )
    return plan, row


def shards(
    velocity, stress, ice_mass, strength, coriolis, air_stress, ocean_current, neighbours, ocean_tile
):
    blocks = velocity.shape[1]
    n = lax.axis_size(("blk", "sub"))
    owners = lax.axis_size("sub")
    cap = max(2, 4 * blocks // n)
    tcap = max(1, 2 * blocks // owners)
    sizes = (n, owners, cap, tcap, blocks)
    cells = velocity.shape[2]
    plan, row = make_plan(neighbours, ocean_tile, sizes, ocean_current.shape[0])
    slots = n * cap
    vmem = pl.BlockSpec(memory_space=pltpu.VMEM)
    dma = pltpu.SemaphoreType.DMA
    return pl.pallas_call(
        functools.partial(kernel, sizes),
        out_shape=(
            jax.ShapeDtypeStruct(velocity.shape, F32),
            jax.ShapeDtypeStruct(stress.shape, F32),
        ),
        in_specs=[pl.BlockSpec(memory_space=pltpu.SMEM)] + [vmem] * 8,
        out_specs=(vmem, vmem),
        scratch_shapes=[
            pltpu.VMEM((2 * blocks, LANES), F32),
            pltpu.VMEM((2 * blocks, LANES), F32),
            pltpu.VMEM((2 * blocks, LANES), F32),
            pltpu.VMEM((2 * blocks, LANES), F32),
            pltpu.VMEM((2, blocks, LANES), F32),
            pltpu.VMEM((2, blocks, LANES), jnp.int32),
            pltpu.SMEM((2 * blocks,), jnp.int32),
            pltpu.VMEM((4, blocks, LANES), F32),
            pltpu.VMEM((n * (cap + 1), 1, LANES), F32),
            pltpu.VMEM((n * (cap + 1) + 1, 1, LANES), F32),
            pltpu.VMEM((n * (cap + 1) + 1, 1, LANES), F32),
            pltpu.VMEM((2 * slots, 1, LANES), F32),
            pltpu.VMEM((2 * slots + 2, 1, LANES), F32),
            pltpu.VMEM((n, 1, LANES), jnp.int32),
            pltpu.SMEM((n, 1, LANES), jnp.int32),
            pltpu.VMEM((owners * tcap, 2, cells), F32),
            pltpu.VMEM((owners * tcap, 2, cells), F32),
            pltpu.VMEM((2, blocks, cells), F32),
            pltpu.VMEM((4, blocks, cells), F32),
            dma((2,)),
            dma((2,)),
            dma,
            dma,
            dma,
            dma,
            dma((owners,)),
            dma((owners,)),
            dma,
        ],
        compiler_params=pltpu.CompilerParams(collective_id=0, has_side_effects=True),
    )(plan, row, velocity, stress, ice_mass, strength, coriolis, air_stress, ocean_current)


def solution(mesh):
    split = ("groups", "blk", "sub")
    placed = (
        P(None, split, None),
        P(None, split, None),
        P(split, None),
        P(split, None),
        P(split, None),
        P(None, split, None),
        P(split, None, None),
        P(split, None),
        P(split),
    )
    return jax.shard_map(
        shards,
        mesh=mesh,
        in_specs=placed,
        out_specs=(P(None, split, None), P(None, split, None)),
        check_vma=False,
    )
```

time: 88.9 us -> 62 us (0.70)
  Pallas kernels: 82.2 us -> 54.1 us
  local copies, waits for them, and re-layouts: 3.95 us -> 5.34 us
    pallas_call x1, Pallas kernels: 82.2 us -> 54.1 us  [shards(): pl.pallas_call(functools.partial(kernel, sizes), out_shape=(jax.ShapeDtyp...]
    unnamed x8 -> x9, local copies, waits for them, and re-layouts: 2.95 us -> 3.59 us
where the time goes in v1:
time: 62 us; the launch traced here: 61.8 us
  Pallas kernels  54.1 us (87%)
  local copies, waits for them, and re-layouts  5.34 us (9%)
  other arithmetic  1.6 us (3%)
  between operations  0.75 us (1%)
    pallas_call x1, Pallas kernels, shards(): pl.pallas_call(functools.partial(kernel, sizes), out_shape=(jax.ShapeDtyp...  54.1 us
    unnamed x9, local copies, waits for them, and re-layouts  3.59 us

profile of v1, /device:TPU:0, one launch (start us, length us, event | category | flops | bytes accessed | tf_op | source)
XLA Modules:
  0.0 61.8 jit_solution(3972059495286816324)
XLA Ops:
  0.7 0.6 %copy-done.2 = s32[16]{0:T(128)S(1)} copy-done((s32[16]{0:T(128)S(1)}, s32[16]{0:T(128)}, u32[]{:S(2)}) %copy-start.2) | copy-done | bytes 88
  1.3 0.2 convert_reduce_fusion.4
  1.5 0.1 select_reduce_fusion.2
  1.6 0.6 copy-done.1
  2.2 0.1 copy.23
  2.3 0.1 reshape.428
  2.4 0.1 pad_add_fusion.1
  2.4 0.5 pad_bitcast_fusion.table_row
  3.0 0.1 reshape.426
  3.2 0.2 convert_reduce_fusion.1
  3.3 0.1 reduce_sum.81
  3.4 0.1 fusion.10
  3.5 0.1 reshape.425
  3.6 0.2 convert_reduce_fusion
  3.9 0.2 convert_reduce_fusion.2
  4.0 0.1 select_reduce_fusion
  4.2 0.2 convert_reduce_fusion.3
  4.3 0.1 select_reduce_fusion.1
  4.4 0.1 reduce_sum.83
  4.6 0.1 reshape.427
  4.7 0.7 %concatenate.10.plan = s32[240]{0:T(256)} concatenate(s32[64]{0:T(128)S(1)} %select_reduce_fusion.1, s32[64]{0:T(128)S(1)} %select_reduce_fusion, s32[64]{0:T(128)S(1)} %reshape.427, s32[32]{0:T(128)S(1)} %add_select_fusion.4, s32[16]{0:T(128)S(1)} %multiply_add_fusion), dimensions={0} | concatenate | bytes 1920 | tf_op jit(solution)/shard_map/concatenate | solution.py:447
  5.4 54.1 %shard_map.104 = (f32[2,16,1024]{2,1,0:T(8,128)}, f32[3,16,1024]{2,1,0:T(8,128)}) custom-call(s32[240]{0:T(256)} %concatenate.10.plan, s32[1,128]{1,0:T(1,128)} %pad_bitcast_fusion.table_row, f32[2,16,1024]{2,1,0:T(8,128)} %vel_in.1, f32[3,16,1024]{2,1,0:T(8,128)} %stress_in.1, f32[16,1024]{1,0:T(8,128)} %mass.1, f32[16,1024]{1,0:T(8,128)} %strength.1, ...), custom_call_target="tpu_custom_call" | custom-call | tf_op jit(solution)/shard_map/pallas_call | solution.py:473
  59.5 1.6 %copy.28 = f32[2,16,1024]{2,1,0:T(8,128)} copy(f32[2,16,1024]{2,1,0:T(8,128)} %get-tuple-element.20) | data formatting | bytes 262144
  61.1 0.7 %copy.29 = f32[3,16,1024]{2,1,0:T(8,128)} copy(f32[3,16,1024]{2,1,0:T(8,128)S(1)} %copy-done) | data formatting | bytes 393216
  (17 shorter events, 0.3 us)
Async XLA Ops:
  0.6 0.7 %copy-start.2 = (s32[16]{0:T(128)S(1)}, s32[16]{0:T(128)}, u32[]{:S(2)}) copy-start(s32[16]{0:T(128)} %param.17) | copy-start | bytes 196
  1.5 0.7 %copy-start.1 = (s32[16,4]{0,1:T(4,128)S(1)}, s32[16,4]{0,1:T(4,128)}, u32[]{:S(2)}) copy-start(s32[16,4]{0,1:T(4,128)} %param.16) | copy-start | bytes 772
  59.5 1.6 %copy-start = (f32[3,16,1024]{2,1,0:T(8,128)S(1)}, f32[3,16,1024]{2,1,0:T(8,128)}, u32[]{:S(2)}) copy-start(f32[3,16,1024]{2,1,0:T(8,128)} %get-tuple-element.21) | copy-start | bytes 589828

commit v2 on v1

--- a/solution.py
+++ b/solution.py
@@ -105,6 +105,7 @@
     ans_recv,
     cur,
     consts,
+    ready,
     send_sem,
     recv_sem,
     h_send_sem,
@@ -259,66 +260,100 @@
         halo[0], halo[1], halo[2] = s1, s2, s12
         return 0.5 * (s1 + s2), 0.5 * (s1 - s2), 0.5 * s12
 
+    def prepare_shifts(here):
+        for c in range(2):
+            x = [here[c, :, chunk(k)] for k in range(CHUNKS)]
+            moved = [roll(y, -SIDE) for y in x]
+            lane = lanes_like(x[0])
+            for k in range(CHUNKS):
+                ready[4 + c, :, chunk(k)] = roll(x[k], -1)
+                north = jnp.where(lane < 96, moved[k], moved[k + 1]) if k + 1 < CHUNKS else moved[k]
+                ready[6 + c, :, chunk(k)] = north
+
+    def prepare_drag(here):
+        for k in range(CHUNKS):
+            u, v = here[0, :, chunk(k)], here[1, :, chunk(k)]
+            uo, vo = cur[0, :, chunk(k)], cur[1, :, chunk(k)]
+            inertia, r, cx, cy = (consts[c, :, chunk(k)] for c in range(4))
+            dx, dy = uo - u, vo - v
+            drag = jnp.sqrt(dx * dx + dy * dy + SPEED_FLOOR)
+            a = inertia + drag
+            inv = 1.0 / (a * a + r * r)
+            ready[0, :, chunk(k)] = a * inv
+            ready[1, :, chunk(k)] = r * inv
+            ready[2, :, chunk(k)] = inertia * u + cx + drag * uo
+            ready[3, :, chunk(k)] = inertia * v + cy + drag * vo
+
     def subcycle(parity, first, last):
         here, old = (vel_in, stress_in) if first else (vel, stress)
         low, high = arrive(parity)
         if first:
-            settle()
+            settle_halo()
         halo_xx, halo_yy, halo_xy = halo_step(high)
         lane = lanes_like(low)
         inner = lane % SIDE
-        us = [here[0, :, chunk(k)] for k in range(CHUNKS)]
-        vs = [here[1, :, chunk(k)] for k in range(CHUNKS)]
-        old_yy, old_xy = row_to(halo_yy, 16, 0), row_to(halo_xy, 16, 0)
-        next_u, next_v = roll(us[0], -SIDE), roll(vs[0], -SIDE)
+        parts = []
         new_u, new_v = [], []
-        for k in range(CHUNKS):
-            u, v = us[k], vs[k]
-            this_u, this_v = next_u, next_v
-            if k + 1 < CHUNKS:
-                next_u, next_v = roll(us[k + 1], -SIDE), roll(vs[k + 1], -SIDE)
-            else:
-                next_u, next_v = row_to(low, 16, 96), row_to(low, 24, 96)
+
+        def stress_chunk(k):
+            u, v = here[0, :, chunk(k)], here[1, :, chunk(k)]
+            u_n, v_n = ready[6, :, chunk(k)], ready[7, :, chunk(k)]
+            if k + 1 == CHUNKS:
+                u_n = jnp.where(lane < 96, u_n, row_to(low, 16, 96))
+                v_n = jnp.where(lane < 96, v_n, row_to(low, 24, 96))
             s1, s2, s12 = advance(
                 [old[c, :, chunk(k)] for c in range(3)],
                 u,
                 v,
-                jnp.where(inner == 31, column_to(low, 0, k, 31), roll(u, -1)),
-                jnp.where(inner == 31, column_to(low, 8, k, 31), roll(v, -1)),
-                jnp.where(lane < 96, this_u, next_u),
-                jnp.where(lane < 96, this_v, next_v),
+                jnp.where(inner == 31, column_to(low, 0, k, 31), ready[4, :, chunk(k)]),
+                jnp.where(inner == 31, column_to(low, 8, k, 31), ready[5, :, chunk(k)]),
+                u_n,
+                v_n,
                 strength[:, chunk(k)],
             )
             stress[0, :, chunk(k)] = s1
             stress[1, :, chunk(k)] = s2
             stress[2, :, chunk(k)] = s12
             xx, yy, xy = 0.5 * (s1 + s2), 0.5 * (s1 - s2), 0.5 * s12
+            parts.append((xx, yy, xy, roll(yy, SIDE), roll(xy, SIDE)))
+
+        def velocity_chunk(k):
+            xx, yy, xy, moved_yy, moved_xy = parts[k]
+            if k:
+                before_yy, before_xy = parts[k - 1][3:]
+            else:
+                before_yy, before_xy = row_to(halo_yy, 16, 0), row_to(halo_xy, 16, 0)
             xx_w = jnp.where(inner == 0, column_to(halo_xx, 0, k, 0), roll(xx, 1))
             xy_w = jnp.where(inner == 0, column_to(halo_xy, 0, k, 0), roll(xy, 1))
-            new_yy, new_xy = roll(yy, SIDE), roll(xy, SIDE)
-            yy_s = jnp.where(lane < SIDE, old_yy, new_yy)
-            xy_s = jnp.where(lane < SIDE, old_xy, new_xy)
-            old_yy, old_xy = new_yy, new_xy
-            force_x = xx - xx_w + xy - xy_s
-            force_y = xy - xy_w + yy - yy_s
-            uo, vo = cur[0, :, chunk(k)], cur[1, :, chunk(k)]
-            inertia, r, cx, cy = (consts[c, :, chunk(k)] for c in range(4))
-            dx, dy = uo - u, vo - v
-            drag = jnp.sqrt(dx * dx + dy * dy + SPEED_FLOOR)
-            a = inertia + drag
-            gx = inertia * u + force_x + cx + drag * uo
-            gy = inertia * v + force_y + cy + drag * vo
-            inv = 1.0 / (a * a + r * r)
-            u, v = (a * gx + r * gy) * inv, (a * gy - r * gx) * inv
+            yy_s = jnp.where(lane < SIDE, before_yy, moved_yy)
+            xy_s = jnp.where(lane < SIDE, before_xy, moved_xy)
+            a, r, gx, gy = (ready[c, :, chunk(k)] for c in range(4))
+            gx = gx + (xx - xx_w + xy - xy_s)
+            gy = gy + (xy - xy_w + yy - yy_s)
+            u, v = a * gx + r * gy, a * gy - r * gx
             vel[0, :, chunk(k)] = u
             vel[1, :, chunk(k)] = v
             new_u.append(u)
             new_v.append(v)
+
+        if first:
+            for k in range(CHUNKS):
+                stress_chunk(k)
+            settle_ocean()
+            prepare_drag(here)
+            for k in range(CHUNKS):
+                velocity_chunk(k)
+        else:
+            for k in range(CHUNKS):
+                stress_chunk(k)
+                velocity_chunk(k)
         wait_all(pack.at[remote], send_sem.at[parity])
         if not last:
             trade(new_u, new_v, 1 - parity)
-
-    def settle():
+            prepare_shifts(vel)
+            prepare_drag(vel)
+
+    def settle_halo():
         wait_all(h_recv.at[pl.ds(2 * cap, 2 * (slots - cap))], h_recv_sem)
         wait_all(h_pack.at[pl.ds(2 * cap, 2 * (slots - cap))], h_send_sem)
         half = lax.broadcasted_iota(jnp.int32, (1, LANES), 1) % SIDE < 16
@@ -329,6 +364,8 @@
         first, second = near[0:blocks], far[0:blocks]
         halo[0], halo[1] = first, roll(first, -8)
         halo[2], halo[3] = second, roll(second, -8)
+
+    def settle_ocean():
         for o in range(1, owners):
             answer_copy(o).wait()
         for b in range(blocks):
@@ -349,28 +386,6 @@
     h_recv[2 * slots] = zero_row
     h_recv[2 * slots + 1] = zero_row
     trade([vel_in[0, :, chunk(k)] for k in range(CHUNKS)], [vel_in[1, :, chunk(k)] for k in range(CHUNKS)], 0)
-
-    s1, s2, s12 = ([stress_in[c, :, chunk(k)] for k in range(CHUNKS)] for c in range(3))
-    p = [strength[:, chunk(k)] for k in range(CHUNKS)]
-    first = gather_edges(s1, s2, s1[-1], s2[-1], 31, 96)
-    second = gather_edges(s12, p, s12[-1], p[-1], 31, 96)
-    for copy in range(2):
-        near[copy * blocks : (copy + 1) * blocks] = first
-        far[copy * blocks : (copy + 1) * blocks] = second
-
-    def fill_halo(o, target):
-        for t in range(cap):
-            s = plan[high_src + o * cap + t]
-            target[2 * (o * cap + t)] = near[pl.ds(s, 1), :]
-            target[2 * (o * cap + t) + 1] = far[pl.ds(s, 1), :]
-
-    def send_halo(o):
-        fill_halo(o, h_pack)
-        where = pl.ds(2 * o * cap, 2 * cap)
-        send_to(o, h_pack.at[where], h_recv.at[where], h_send_sem, h_recv_sem, peer(o)).start()
-
-    repeat(1, n, send_halo)
-    fill_halo(0, h_recv)
 
     table[0] = table_row[...]
     wait_all(table.at[pl.ds(1, n - 1)], t_recv_sem)
@@ -386,6 +401,28 @@
             (ans_pack if o else ans_recv)[o * tcap + t] = tile
         if o:
             answer_copy(o).start()
+    s1, s2, s12 = ([stress_in[c, :, chunk(k)] for k in range(CHUNKS)] for c in range(3))
+    p = [strength[:, chunk(k)] for k in range(CHUNKS)]
+    first = gather_edges(s1, s2, s1[-1], s2[-1], 31, 96)
+    second = gather_edges(s12, p, s12[-1], p[-1], 31, 96)
+    for copy in range(2):
+        near[copy * blocks : (copy + 1) * blocks] = first
+        far[copy * blocks : (copy + 1) * blocks] = second
+
+    def fill_halo(o, target):
+        for t in range(cap):
+            s = plan[high_src + o * cap + t]
+            target[2 * (o * cap + t)] = near[pl.ds(s, 1), :]
+            target[2 * (o * cap + t) + 1] = far[pl.ds(s, 1), :]
+
+    def send_halo(o):
+        fill_halo(o, h_pack)
+        where = pl.ds(2 * o * cap, 2 * cap)
+        send_to(o, h_pack.at[where], h_recv.at[where], h_send_sem, h_recv_sem, peer(o)).start()
+
+    repeat(1, n, send_halo)
+    fill_halo(0, h_recv)
+
     for b in range(blocks):
         for which in range(2):
             via = jnp.maximum(table_s[0, 0, 4 * b + which], 0)
@@ -397,6 +434,7 @@
             corner_slot[which * blocks + b] = jnp.where(known, slot, zero_slot)
             corner_lane[which, pl.ds(b, 1), :] = jnp.full((1, LANES), lax.rem(far_block, blocks), jnp.int32)
 
+    prepare_shifts(vel_in)
     subcycle(0, True, False)
 
     def pair(_, carry):
@@ -498,6 +536,7 @@
             pltpu.VMEM((owners * tcap, 2, cells), F32),
             pltpu.VMEM((2, blocks, cells), F32),
             pltpu.VMEM((4, blocks, cells), F32),
+            pltpu.VMEM((8, blocks, cells), F32),
             dma((2,)),
             dma((2,)),
             dma,

time: 62 us -> 63 us (1.016)
  Pallas kernels: 54.1 us -> 55.1 us
    pallas_call x1, Pallas kernels: 54.1 us -> 55.1 us  [shards(): pl.pallas_call(functools.partial(kernel, sizes), out_shape=(jax.ShapeDtyp...]
where the time goes in v2:
time: 63 us; the launch traced here: 62.8 us
  Pallas kernels  55.1 us (87%)
  local copies, waits for them, and re-layouts  5.34 us (8%)
  other arithmetic  1.6 us (3%)
  between operations  0.75 us (1%)
    pallas_call x1, Pallas kernels, shards(): pl.pallas_call(functools.partial(kernel, sizes), out_shape=(jax.ShapeDtyp...  55.1 us
    unnamed x9, local copies, waits for them, and re-layouts  3.59 us

profile of v2, /device:TPU:0, one launch (start us, length us, event | category | flops | bytes accessed | tf_op | source)
XLA Modules:
  0.0 62.8 jit_solution(12461772898571831419)
XLA Ops:
  0.7 0.6 %copy-done.2 = s32[16]{0:T(128)S(1)} copy-done((s32[16]{0:T(128)S(1)}, s32[16]{0:T(128)}, u32[]{:S(2)}) %copy-start.2) | copy-done | bytes 88
  1.3 0.2 convert_reduce_fusion.4
  1.5 0.1 select_reduce_fusion.2
  1.6 0.6 copy-done.1
  2.2 0.1 copy.23
  2.3 0.1 reshape.428
  2.4 0.1 pad_add_fusion.1
  2.4 0.5 pad_bitcast_fusion.table_row
  3.0 0.1 reshape.426
  3.2 0.2 convert_reduce_fusion.1
  3.3 0.1 reduce_sum.81
  3.4 0.1 fusion.10
  3.5 0.1 reshape.425
  3.6 0.2 convert_reduce_fusion
  3.9 0.2 convert_reduce_fusion.2
  4.0 0.1 select_reduce_fusion
  4.2 0.2 convert_reduce_fusion.3
  4.3 0.1 select_reduce_fusion.1
  4.4 0.1 reduce_sum.83
  4.6 0.1 reshape.427
  4.7 0.7 %concatenate.10.plan = s32[240]{0:T(256)} concatenate(s32[64]{0:T(128)S(1)} %select_reduce_fusion.1, s32[64]{0:T(128)S(1)} %select_reduce_fusion, s32[64]{0:T(128)S(1)} %reshape.427, s32[32]{0:T(128)S(1)} %add_select_fusion.4, s32[16]{0:T(128)S(1)} %multiply_add_fusion), dimensions={0} | concatenate | bytes 1920 | tf_op jit(solution)/shard_map/concatenate | solution.py:485
  5.4 55.1 %shard_map.104 = (f32[2,16,1024]{2,1,0:T(8,128)}, f32[3,16,1024]{2,1,0:T(8,128)}) custom-call(s32[240]{0:T(256)} %concatenate.10.plan, s32[1,128]{1,0:T(1,128)} %pad_bitcast_fusion.table_row, f32[2,16,1024]{2,1,0:T(8,128)} %vel_in.1, f32[3,16,1024]{2,1,0:T(8,128)} %stress_in.1, f32[16,1024]{1,0:T(8,128)} %mass.1, f32[16,1024]{1,0:T(8,128)} %strength.1, ...), custom_call_target="tpu_custom_call" | custom-call | tf_op jit(solution)/shard_map/pallas_call | solution.py:511
  60.5 1.6 %copy.28 = f32[2,16,1024]{2,1,0:T(8,128)} copy(f32[2,16,1024]{2,1,0:T(8,128)} %get-tuple-element.20) | data formatting | bytes 262144
  62.1 0.7 %copy.29 = f32[3,16,1024]{2,1,0:T(8,128)} copy(f32[3,16,1024]{2,1,0:T(8,128)S(1)} %copy-done) | data formatting | bytes 393216
  (17 shorter events, 0.3 us)
Async XLA Ops:
  0.6 0.7 %copy-start.2 = (s32[16]{0:T(128)S(1)}, s32[16]{0:T(128)}, u32[]{:S(2)}) copy-start(s32[16]{0:T(128)} %param.17) | copy-start | bytes 196
  1.5 0.7 %copy-start.1 = (s32[16,4]{0,1:T(4,128)S(1)}, s32[16,4]{0,1:T(4,128)}, u32[]{:S(2)}) copy-start(s32[16,4]{0,1:T(4,128)} %param.16) | copy-start | bytes 772
  60.5 1.6 %copy-start = (f32[3,16,1024]{2,1,0:T(8,128)S(1)}, f32[3,16,1024]{2,1,0:T(8,128)}, u32[]{:S(2)}) copy-start(f32[3,16,1024]{2,1,0:T(8,128)} %get-tuple-element.21) | copy-start | bytes 589828

commit v3 on v2

--- a/solution.py
+++ b/solution.py
@@ -387,6 +387,28 @@
     h_recv[2 * slots + 1] = zero_row
     trade([vel_in[0, :, chunk(k)] for k in range(CHUNKS)], [vel_in[1, :, chunk(k)] for k in range(CHUNKS)], 0)
 
+    s1, s2, s12 = ([stress_in[c, :, chunk(k)] for k in range(CHUNKS)] for c in range(3))
+    p = [strength[:, chunk(k)] for k in range(CHUNKS)]
+    first = gather_edges(s1, s2, s1[-1], s2[-1], 31, 96)
+    second = gather_edges(s12, p, s12[-1], p[-1], 31, 96)
+    for copy in range(2):
+        near[copy * blocks : (copy + 1) * blocks] = first
+        far[copy * blocks : (copy + 1) * blocks] = second
+
+    def fill_halo(o, target):
+        for t in range(cap):
+            s = plan[high_src + o * cap + t]
+            target[2 * (o * cap + t)] = near[pl.ds(s, 1), :]
+            target[2 * (o * cap + t) + 1] = far[pl.ds(s, 1), :]
+
+    def send_halo(o):
+        fill_halo(o, h_pack)
+        where = pl.ds(2 * o * cap, 2 * cap)
+        send_to(o, h_pack.at[where], h_recv.at[where], h_send_sem, h_recv_sem, peer(o)).start()
+
+    repeat(1, n, send_halo)
+    fill_halo(0, h_recv)
+
     table[0] = table_row[...]
     wait_all(table.at[pl.ds(1, n - 1)], t_recv_sem)
     wait_all(table.at[pl.ds(1, n - 1)], t_send_sem)
@@ -401,28 +423,6 @@
             (ans_pack if o else ans_recv)[o * tcap + t] = tile
         if o:
             answer_copy(o).start()
-    s1, s2, s12 = ([stress_in[c, :, chunk(k)] for k in range(CHUNKS)] for c in range(3))
-    p = [strength[:, chunk(k)] for k in range(CHUNKS)]
-    first = gather_edges(s1, s2, s1[-1], s2[-1], 31, 96)
-    second = gather_edges(s12, p, s12[-1], p[-1], 31, 96)
-    for copy in range(2):
-        near[copy * blocks : (copy + 1) * blocks] = first
-        far[copy * blocks : (copy + 1) * blocks] = second
-
-    def fill_halo(o, target):
-        for t in range(cap):
-            s = plan[high_src + o * cap + t]
-            target[2 * (o * cap + t)] = near[pl.ds(s, 1), :]
-            target[2 * (o * cap + t) + 1] = far[pl.ds(s, 1), :]
-
-    def send_halo(o):
-        fill_halo(o, h_pack)
-        where = pl.ds(2 * o * cap, 2 * cap)
-        send_to(o, h_pack.at[where], h_recv.at[where], h_send_sem, h_recv_sem, peer(o)).start()
-
-    repeat(1, n, send_halo)
-    fill_halo(0, h_recv)
-
     for b in range(blocks):
         for which in range(2):
             via = jnp.maximum(table_s[0, 0, 4 * b + which], 0)

time: 63 us -> 60.5 us (0.960)
  Pallas kernels: 55.1 us -> 52.6 us
    pallas_call x1, Pallas kernels: 55.1 us -> 52.6 us  [shards(): pl.pallas_call(functools.partial(kernel, sizes), out_shape=(jax.ShapeDtyp...]
where the time goes in v3:
time: 60.5 us; the launch traced here: 60.3 us
  Pallas kernels  52.6 us (87%)
  local copies, waits for them, and re-layouts  5.34 us (9%)
  other arithmetic  1.6 us (3%)
  between operations  0.75 us (1%)
    pallas_call x1, Pallas kernels, shards(): pl.pallas_call(functools.partial(kernel, sizes), out_shape=(jax.ShapeDtyp...  52.6 us
    unnamed x9, local copies, waits for them, and re-layouts  3.59 us

profile of v3, /device:TPU:0, one launch (start us, length us, event | category | flops | bytes accessed | tf_op | source)
XLA Modules:
  0.0 60.3 jit_solution(13758438988258645727)
XLA Ops:
  0.7 0.6 %copy-done.2 = s32[16]{0:T(128)S(1)} copy-done((s32[16]{0:T(128)S(1)}, s32[16]{0:T(128)}, u32[]{:S(2)}) %copy-start.2) | copy-done | bytes 88
  1.3 0.2 convert_reduce_fusion.4
  1.5 0.1 select_reduce_fusion.2
  1.6 0.6 copy-done.1
  2.2 0.1 copy.23
  2.3 0.1 reshape.428
  2.4 0.1 pad_add_fusion.1
  2.4 0.5 pad_bitcast_fusion.table_row
  3.0 0.1 reshape.426
  3.2 0.2 convert_reduce_fusion.1
  3.3 0.1 reduce_sum.81
  3.4 0.1 fusion.10
  3.5 0.1 reshape.425
  3.6 0.2 convert_reduce_fusion
  3.9 0.2 convert_reduce_fusion.2
  4.0 0.1 select_reduce_fusion
  4.2 0.2 convert_reduce_fusion.3
  4.3 0.1 select_reduce_fusion.1
  4.4 0.1 reduce_sum.83
  4.6 0.1 reshape.427
  4.7 0.7 %concatenate.10.plan = s32[240]{0:T(256)} concatenate(s32[64]{0:T(128)S(1)} %select_reduce_fusion.1, s32[64]{0:T(128)S(1)} %select_reduce_fusion, s32[64]{0:T(128)S(1)} %reshape.427, s32[32]{0:T(128)S(1)} %add_select_fusion.4, s32[16]{0:T(128)S(1)} %multiply_add_fusion), dimensions={0} | concatenate | bytes 1920 | tf_op jit(solution)/shard_map/concatenate | solution.py:485
  5.4 52.6 %shard_map.104 = (f32[2,16,1024]{2,1,0:T(8,128)}, f32[3,16,1024]{2,1,0:T(8,128)}) custom-call(s32[240]{0:T(256)} %concatenate.10.plan, s32[1,128]{1,0:T(1,128)} %pad_bitcast_fusion.table_row, f32[2,16,1024]{2,1,0:T(8,128)} %vel_in.1, f32[3,16,1024]{2,1,0:T(8,128)} %stress_in.1, f32[16,1024]{1,0:T(8,128)} %mass.1, f32[16,1024]{1,0:T(8,128)} %strength.1, ...), custom_call_target="tpu_custom_call" | custom-call | tf_op jit(solution)/shard_map/pallas_call | solution.py:511
  58.0 1.6 %copy.28 = f32[2,16,1024]{2,1,0:T(8,128)} copy(f32[2,16,1024]{2,1,0:T(8,128)} %get-tuple-element.20) | data formatting | bytes 262144
  59.6 0.7 %copy.29 = f32[3,16,1024]{2,1,0:T(8,128)} copy(f32[3,16,1024]{2,1,0:T(8,128)S(1)} %copy-done) | data formatting | bytes 393216
  (17 shorter events, 0.3 us)
Async XLA Ops:
  0.6 0.7 %copy-start.2 = (s32[16]{0:T(128)S(1)}, s32[16]{0:T(128)}, u32[]{:S(2)}) copy-start(s32[16]{0:T(128)} %param.17) | copy-start | bytes 196
  1.5 0.7 %copy-start.1 = (s32[16,4]{0,1:T(4,128)S(1)}, s32[16,4]{0,1:T(4,128)}, u32[]{:S(2)}) copy-start(s32[16,4]{0,1:T(4,128)} %param.16) | copy-start | bytes 772
  58.0 1.6 %copy-start = (f32[3,16,1024]{2,1,0:T(8,128)S(1)}, f32[3,16,1024]{2,1,0:T(8,128)}, u32[]{:S(2)}) copy-start(f32[3,16,1024]{2,1,0:T(8,128)} %get-tuple-element.21) | copy-start | bytes 589828
